TPU v7x, 32 devices: a whole 2x2x4 slice. The times are simulated.
32 devices in a mesh: atom: 4 (over y, x), mode: 8 (over z, core).
Axes of the slice: x: 2, y: 2, z: 4, core: 2. Of those that a mesh axis runs over, the one named last changes fastest.
Arguments:
- first_panel: bfloat16 [16384, 3, 1024], P('atom', None, 'mode'), may hold values from -6 to 6
- second_panel: bfloat16 [16384, 3, 1024], P('atom', None, 'mode'), may hold values from -6 to 6
- offsets: int32 [24, 16384], P(None, 'atom'), may hold values from -256 to 256, as said below
- forces: float32 [24, 3, 3, 16384], P(None, None, None, 'atom'), may hold values from -0.75 to 0.75
- displacements: float32 [24, 3, 16384], P(None, None, 'atom'), may hold values from -1 to 1
Outputs:
- velocity: float32 [1024, 3, 1024], P(('atom', 'mode'))
Inputs may be any that keep to these rules, and one draw needn't show every extreme that they name: `offsets`: no entry is zero, and both 256 and -256 occur.
All inputs are finite; a program needn't handle non-finite values.
Results may differ from a plain program's by a relative error of at most 0.0041.
Values may be sent and summed in bfloat16 or wider, within the bound.
A program may use at most 192 MiB of HBM per device.

v0:
```python
import jax
import jax.numpy as jnp
from jax import lax
from jax.sharding import PartitionSpec as P


def padded_2(block, sides, width):
    for axis, dim in sides:
        count = lax.axis_size(axis)
        forward = [(i, i + 1) for i in range(count - 1)]
        forward.append((count - 1, 0))
        backward = [(target, source) for source, target in forward]
        low = lax.ppermute(
            lax.slice_in_dim(block, block.shape[dim] - width, None, axis=dim), axis, forward
        )
        high = lax.ppermute(lax.slice_in_dim(block, 0, width, axis=dim), axis, backward)
        block = jnp.concatenate([low, block, high], axis=dim)
    return block


def make_images(padded, shifts, force_part, disp_part, rim_width):
    row_total = shifts.shape[1]
    block_rows = 128
    columns = padded.shape[2]

    def one_block(number):
        row_start = number * block_rows
        local_shifts = lax.dynamic_slice_in_dim(shifts, row_start, block_rows, 1)
        positions = (
            row_start + jnp.arange(block_rows, dtype=jnp.int32)[None, :] + rim_width + local_shifts
        )
        gathered = padded[positions]
        local_forces = lax.dynamic_slice_in_dim(force_part, row_start, block_rows, 3)
        local_disp = lax.dynamic_slice_in_dim(disp_part, row_start, block_rows, 2)
        blocks = (local_disp[:, :, None, None, :] * local_forces[:, None, :, :, :]).astype(
            jnp.bfloat16
        )
        result = jnp.einsum(
            "kqabi,kibn->iqan", blocks, gathered, preferred_element_type=jnp.float32
        )
        return result.astype(jnp.bfloat16)

    stacked = lax.map(one_block, jnp.arange(row_total // block_rows, dtype=jnp.int32))
    return stacked.reshape(row_total, 3, 3, columns)


def body(first_panel, second_panel, offsets, forces, displacements):
    rows_dom = first_panel.shape[0]
    groups = lax.axis_size("mode")
    rows_dev = rows_dom // groups
    rim_width = rows_dev // 2
    atoms_all = rows_dom * lax.axis_size("atom")
    factor = 1.0 / (3.0 * atoms_all) ** 0.5
    panel_rows, second_rows = (
        lax.all_to_all(first_panel, "mode", split_axis=0, concat_axis=2, tiled=True),
        lax.all_to_all(second_panel, "mode", split_axis=0, concat_axis=2, tiled=True),
    )
    padded = padded_2(second_rows, ((("atom", "mode"), 0),), rim_width)
    row_start = lax.axis_index("mode") * rows_dev
    shifts = lax.dynamic_slice_in_dim(offsets, row_start, rows_dev, 1)
    force_part = lax.dynamic_slice_in_dim(forces, row_start, rows_dev, 3)
    disp_part = lax.dynamic_slice_in_dim(displacements, row_start, rows_dev, 2)
    images = make_images(padded, shifts, force_part, disp_part, rim_width)
    product = jnp.einsum("iam,iqan->mqn", panel_rows, images, preferred_element_type=jnp.float32)
    return lax.psum_scatter(product * factor, ("atom", "mode"), scatter_dimension=0, tiled=True)


def solution(mesh):
    in_specs = (
        P("atom", None, "mode"),
        P("atom", None, "mode"),
        P(None, "atom"),
        P(None, None, None, "atom"),
        P(None, None, "atom"),
    )
    out_specs = P(("atom", "mode"), None, None)
    return jax.shard_map(body, mesh=mesh, in_specs=in_specs, out_specs=out_specs, check_vma=False)
```

profile of v0, /device:TPU:10, one launch (start us, length us, event | category | flops | bytes accessed | tf_op | source)
XLA Modules:
  0.0 909.8 jit_solution(2311252396583939107)
XLA Ops:
  6.5 6.9 copy.33
  13.5 5.3 all-to-all-start
  18.8 6.8 copy.39
  25.6 83.8 %all-to-all-done = bf16[4096,3,128]{2,1,0:T(4,128)(2,1)} async-done(((bf16[4096,3,128]{2,1,0:T(4,128)(2,1)}), bf16[4096,3,128]{2,1,0:T(4,128)(2,1)}, u32[]{:S(2)}, u32[]{:S(2)}) %all-to-all-start) | async-done | bytes 3145760 | tf_op jit(solution)/shard_map/all_to_all | solution.py:56
  109.3 8.0 all-to-all-start.1
  117.3 2.6 copy.34
  134.4 4.6 copy.36
  139.0 85.8 %all-to-all-done.1 = bf16[4096,3,128]{2,1,0:T(4,128)(2,1)} async-done(((bf16[4096,3,128]{2,1,0:T(4,128)(2,1)}), bf16[4096,3,128]{2,1,0:T(4,128)(2,1)}, u32[]{:S(2)}, u32[]{:S(2)}) %all-to-all-start.1) | async-done | bytes 3145760 | tf_op jit(solution)/shard_map/all_to_all | solution.py:55
  224.8 4.8 copy.62
  229.5 3.4 reshape.29
  232.9 6.5 pad_maximum_fusion
  239.4 14.4 %copy.38 = bf16[1024,3,1024]{2,1,0:T(4,128)(2,1)} copy(bf16[1024,3,1024]{0,2,1:T(8,128)(2,1)} %pad_maximum_fusion) | data formatting | bytes 12582912 | tf_op jit(solution)/shard_map/while | solution.py:43
  253.8 320.0 %while.10 = (s32[]{:T(128)}, bf16[4,128,3,3,1024]{4,3,2,1,0:T(4,128)(2,1)}, s32[4]{0:T(128)S(1)}, f32[24,3,512]{2,0,1:T(8,128)}, f32[24,3,3,512]{3,0,2,1:T(8,128...) while((s32[]{:T(128)}, ...), condition=%wide.region_1.2_spmd, body=%wide.region_0.1_spmd.sunk | while | flops 171230464 | bytes 66836152 | solution.py:43
  255.8 48.5 %gather_fusion = bf16[3072,3,1024]{2,1,0:T(4,128)(2,1)} fusion(bf16[1024,3,1024]{2,1,0:T(4,128)(2,1)} %get-tuple-element.151, s32[3072]{0:T(1024)S(1)} %fusion.21), kind=kCustom, calls=%fused_computation.clone.1 | custom fusion | bytes 37761024 | tf_op jit(solution)/shard_map/while/body/eval_jaxpr/gather | solution.py:32
  306.4 27.3 %fusion.22 = bf16[4,128,3,3,1024]{4,3,2,1,0:T(4,128)(2,1)} fusion(bf16[4,128,3,3,1024]{4,3,2,1,0:T(4,128)(2,1)} %get-tuple-element.135, s32[]{:T(128)} %get-tuple-element.134, bf16[24,128,3,1024,1]{3,2,1,0,4:T(4,128)(2,1)} %bitcast.52, f32[24,3,3,128]{0,1,2,3:T(4,128)S(1)} %copy.67, f32[24,3,128]{0,1,2:T(4,128)S(1)} %copy.68), kind=kOutput, calls=%fused_computation.5.clone.1 | convolution fusion | flops 171214848 | bytes 28459520 | tf_op jit(solution)/shard_map/while/body/eval_jaxpr/kqabi,kibn->iqan/dot_general | solution.py:38
  335.8 48.5 %gather_fusion = bf16[3072,3,1024]{2,1,0:T(4,128)(2,1)} fusion(bf16[1024,3,1024]{2,1,0:T(4,128)(2,1)} %get-tuple-element.151, s32[3072]{0:T(1024)S(1)} %fusion.21), kind=kCustom, calls=%fused_computation.clone.1 | custom fusion | bytes 37761024 | tf_op jit(solution)/shard_map/while/body/eval_jaxpr/gather | solution.py:32
  386.4 27.4 %fusion.22 = bf16[4,128,3,3,1024]{4,3,2,1,0:T(4,128)(2,1)} fusion(bf16[4,128,3,3,1024]{4,3,2,1,0:T(4,128)(2,1)} %get-tuple-element.135, s32[]{:T(128)} %get-tuple-element.134, bf16[24,128,3,1024,1]{3,2,1,0,4:T(4,128)(2,1)} %bitcast.52, f32[24,3,3,128]{0,1,2,3:T(4,128)S(1)} %copy.67, f32[24,3,128]{0,1,2:T(4,128)S(1)} %copy.68), kind=kOutput, calls=%fused_computation.5.clone.1 | convolution fusion | flops 171214848 | bytes 28459520 | tf_op jit(solution)/shard_map/while/body/eval_jaxpr/kqabi,kibn->iqan/dot_general | solution.py:38
  415.8 48.5 %gather_fusion = bf16[3072,3,1024]{2,1,0:T(4,128)(2,1)} fusion(bf16[1024,3,1024]{2,1,0:T(4,128)(2,1)} %get-tuple-element.151, s32[3072]{0:T(1024)S(1)} %fusion.21), kind=kCustom, calls=%fused_computation.clone.1 | custom fusion | bytes 37761024 | tf_op jit(solution)/shard_map/while/body/eval_jaxpr/gather | solution.py:32
  466.4 27.4 %fusion.22 = bf16[4,128,3,3,1024]{4,3,2,1,0:T(4,128)(2,1)} fusion(bf16[4,128,3,3,1024]{4,3,2,1,0:T(4,128)(2,1)} %get-tuple-element.135, s32[]{:T(128)} %get-tuple-element.134, bf16[24,128,3,1024,1]{3,2,1,0,4:T(4,128)(2,1)} %bitcast.52, f32[24,3,3,128]{0,1,2,3:T(4,128)S(1)} %copy.67, f32[24,3,128]{0,1,2:T(4,128)S(1)} %copy.68), kind=kOutput, calls=%fused_computation.5.clone.1 | convolution fusion | flops 171214848 | bytes 28459520 | tf_op jit(solution)/shard_map/while/body/eval_jaxpr/kqabi,kibn->iqan/dot_general | solution.py:38
  495.8 48.5 %gather_fusion = bf16[3072,3,1024]{2,1,0:T(4,128)(2,1)} fusion(bf16[1024,3,1024]{2,1,0:T(4,128)(2,1)} %get-tuple-element.151, s32[3072]{0:T(1024)S(1)} %fusion.21), kind=kCustom, calls=%fused_computation.clone.1 | custom fusion | bytes 37761024 | tf_op jit(solution)/shard_map/while/body/eval_jaxpr/gather | solution.py:32
  546.5 27.4 %fusion.22 = bf16[4,128,3,3,1024]{4,3,2,1,0:T(4,128)(2,1)} fusion(bf16[4,128,3,3,1024]{4,3,2,1,0:T(4,128)(2,1)} %get-tuple-element.135, s32[]{:T(128)} %get-tuple-element.134, bf16[24,128,3,1024,1]{3,2,1,0,4:T(4,128)(2,1)} %bitcast.52, f32[24,3,3,128]{0,1,2,3:T(4,128)S(1)} %copy.67, f32[24,3,128]{0,1,2:T(4,128)S(1)} %copy.68), kind=kOutput, calls=%fused_computation.5.clone.1 | convolution fusion | flops 171214848 | bytes 28459520 | tf_op jit(solution)/shard_map/while/body/eval_jaxpr/kqabi,kibn->iqan/dot_general | solution.py:38
  573.8 20.7 %fusion.10 = f32[1024,3,1024]{0,2,1:T(8,128)} fusion(bf16[512,3,1024,1]{2,0,1,3:T(8,128)(2,1)} %reshape.29, bf16[512,3,3,1024]{3,2,1,0:T(4,128)(2,1)} %bitcast.59), kind=kOutput, calls=%fused_computation.16 | convolution fusion | flops 9666822144 | bytes 25165824 | tf_op jit(solution)/shard_map/iam,iqan->mqn/dot_general | solution.py:64
  594.5 18.4 %copy.42 = f32[1024,3,1024]{2,1,0:T(4,128)} copy(f32[1024,3,1024]{0,2,1:T(8,128)} %fusion.10) | data formatting | bytes 25165824 | tf_op jit(solution)/shard_map/mul | solution.py:65
  612.9 287.9 %all-reduce.3.cloned.1.call-done = f32[1024,3,1024]{2,1,0:T(4,128)} async-done(((f32[1024,3,1024]{2,1,0:T(4,128)}), f32[1024,3,1024]{2,1,0:T(4,128)}) %all-reduce.3.cloned.1.call-update) | async-done | bytes 12582928
  (50 shorter events, 30.5 us)
Async XLA Ops:
  6.5 127.0 %copy-start = (f32[24,3,3,4096]{3,0,2,1:T(8,128)S(1)}, f32[24,3,3,4096]{3,0,2,1:T(8,128)}, u32[]{:S(2)}) copy-start(f32[24,3,3,4096]{3,0,2,1:T(8,128)} %param.10) | copy-start | bytes 10616836
  13.5 95.9 %all-to-all-start = ((bf16[4096,3,128]{2,1,0:T(4,128)(2,1)}), bf16[4096,3,128]{2,1,0:T(4,128)(2,1)}, u32[]{:S(2)}, u32[]{:S(2)}) async-start(bf16[4096,3,128]{2,1,0:T(4,128)(2,1)} %copy.33), calls=%async_computation | async-start | bytes 8388608 | tf_op jit(solution)/shard_map/all_to_all | solution.py:56
  109.3 115.4 %all-to-all-start.1 = ((bf16[4096,3,128]{2,1,0:T(4,128)(2,1)}), bf16[4096,3,128]{2,1,0:T(4,128)(2,1)}, u32[]{:S(2)}, u32[]{:S(2)}) async-start(bf16[4096,3,128]{2,1,0:T(4,128)(2,1)} %copy.39), calls=%async_computation.1 | async-start | bytes 8388608 | tf_op jit(solution)/shard_map/all_to_all | solution.py:55
  117.3 783.5 %all-reduce.3.cloned.1.call-start = ((), (), s32[]{:S(2)}) async-start(), calls=%async_computation.2 | async-start | bytes 33554432
  120.0 1.6 copy-start.2
  126.2 106.7 %collective-permute-start = (bf16[256,3,1024]{0,2,1:T(8,128)(2,1)}, bf16[256,3,1024]{0,2,1:T(8,128)(2,1)}, u32[]{:S(2)}, u32[]{:S(2)}) collective-permute-start(bf16[256,3,1024]{0,2,1:T(8,128)(2,1)} %bitcast.57), channel_id=1, source_target_pairs={{0,1},{1,2},{2,3},{3,4},{4,5},{5,6},{6,7},{7,8},{8,9},{9,10},{10,1... | collective-permute-start | bytes 4718600 | tf_op jit(solution)/shard_map/ppermute | solution.py:13
  129.0 103.9 %collective-permute-start.1 = (bf16[256,3,1024]{0,2,1:T(8,128)(2,1)}, bf16[256,3,1024]{0,2,1:T(8,128)(2,1)}, u32[]{:S(2)}, u32[]{:S(2)}) collective-permute-start(bf16[256,3,1024]{0,2,1:T(8,128)(2,1)} %bitcast.58), channel_id=1, source_target_pairs={{1,0},{2,1},{3,2},{4,3},{5,4},{6,5},{7,6},{8,7},{9,8},{10,9},{11,1... | collective-permute-start | bytes 4718600 | tf_op jit(solution)/shard_map/ppermute | solution.py:16
  612.9 290.0 %copy-start.1 = (f32[24,3,3,4096]{3,0,2,1:T(8,128)S(1)}, f32[24,3,3,4096]{3,0,2,1:T(8,128)}, u32[]{:S(2)}) copy-start(f32[24,3,3,4096]{3,0,2,1:T(8,128)} %param.10) | copy-start | bytes 10616836
Sparse Core Ops, SparseCore 0:
  613.0 287.7 all-reduce.2
where the time goes:
time: 914 us; the launch traced here: 910 us
  waiting for transfers between devices  457 us (50%)
  local copies, waits for them, and re-layouts  282 us (31%)
  matrix products  130 us (14%)
  starting transfers between devices  15.1 us (2%)
  between operations  13.4 us (1%)
  other arithmetic  9.43 us (1%)
    unnamed x2, waiting for transfers between devices  288 us
    gather x4, local copies, waits for them, and re-layouts, one_block(): gathered = padded[positions]  194 us
    dot_general x4, matrix products, one_block(): jnp.einsum('kqabi,kibn->iqan', blocks, gathered, preferred_element_type=j...  109 us
    all_to_all x1, waiting for transfers between devices, body(): lax.all_to_all(first_panel, 'mode', split_axis=0, concat_axis=2, tiled=True)  85.8 us
    all_to_all x1, waiting for transfers between devices, body(): lax.all_to_all(second_panel, 'mode', split_axis=0, concat_axis=2, tiled=T...  83.8 us
    dot_general x1, matrix products, body(): jnp.einsum('iam,iqan->mqn', panel_rows, images, preferred_element_type=jn...  20.7 us
    mul x1, local copies, waits for them, and re-layouts, body(): product * factor  18.4 us
  transfers between devices with their start and end apart: 5, of which 3 were waited for; matrix products, arithmetic and copies ran while one was open for 4% of the time, Pallas kernels for 0%

commit v1 on v0

v1 whole, which is shorter than its diff:
```python
import functools

import jax
import jax.numpy as jnp
from jax import lax
from jax.experimental import pallas as pl
from jax.experimental.pallas import tpu as pltpu
from jax.sharding import PartitionSpec as P

RIM = 256
BLOCK = 128
CHUNK = 64
MESH = pl.DeviceIdType.MESH


def with_rims(block, width):
    axes = ("atom", "mode")
    count = lax.axis_size(axes)
    forward = [(i, (i + 1) % count) for i in range(count)]
    backward = [(target, source) for source, target in forward]
    low = lax.ppermute(block[:, block.shape[1] - width :], axes, forward)
    high = lax.ppermute(block[:, :width], axes, backward)
    return jnp.concatenate([low, block, high], axis=1)


def merged_blocks(offsets, forces, displacements):
    slots, rows = offsets.shape
    blocks = displacements[:, :, None, None, :] * forces[:, None, :, :, :]
    blocks = blocks.astype(jnp.bfloat16).astype(jnp.float32).reshape(slots, 9, 3, rows)
    same = offsets[:, None, :] == offsets[None, :, :]
    merged = jnp.sum(
        jnp.where(same[:, :, None, None, :], blocks[None], 0.0), axis=1
    )
    return merged.transpose(1, 0, 2, 3).reshape(9, slots * 3, rows)


def image_kernel(slots, offs_ref, coef_ref, s_ref, out_ref, w_ref):
    window = BLOCK + 2 * RIM
    start = pl.multiple_of(pl.program_id(0) * BLOCK, BLOCK)
    target = offs_ref[...] + lax.broadcasted_iota(jnp.int32, offs_ref.shape, 1) + RIM
    rows = lax.broadcasted_iota(jnp.int32, (CHUNK, BLOCK), 0)

    for qa in range(9):

        @pl.loop(0, window // CHUNK)
        def _(c):
            at = pl.multiple_of(c * CHUNK, CHUNK)
            here = rows + at
            acc = [jnp.zeros((CHUNK, BLOCK), jnp.float32) for _ in range(3)]
            for k in range(slots):
                hit = here == target[k : k + 1, :]
                for b in range(3):
                    row = coef_ref[qa, 3 * k + b : 3 * k + b + 1, :]
                    acc[b] = jnp.where(hit, row, acc[b])
            for b in range(3):
                w_ref[b, pl.ds(at, CHUNK), qa * BLOCK : (qa + 1) * BLOCK] = acc[b].astype(
                    jnp.bfloat16
                )

    columns = s_ref.shape[2]
    wide = 512

    @pl.loop(0, columns // wide)
    def _(c):
        at = pl.multiple_of(c * wide, wide)
        total = None
        for b in range(3):
            term = lax.dot_general(
                w_ref[b],
                s_ref[b, pl.ds(start, window), pl.ds(at, wide)],
                (((0,), (0,)), ((), ())),
                preferred_element_type=jnp.float32,
            )
            total = term if total is None else total + term
        out_ref[:, :, pl.ds(at, wide)] = total.astype(jnp.bfloat16).reshape(9, BLOCK, wide)


def make_images(padded, offs, coef):
    slots, rows = offs.shape
    columns = padded.shape[2]
    window = BLOCK + 2 * RIM
    return pl.pallas_call(
        functools.partial(image_kernel, slots),
        grid=(rows // BLOCK,),
        out_shape=jax.ShapeDtypeStruct((9, rows, columns), jnp.bfloat16),
        in_specs=[
            pl.BlockSpec((slots, BLOCK), lambda i: (0, i)),
            pl.BlockSpec((9, slots * 3, BLOCK), lambda i: (0, 0, i)),
            pl.BlockSpec(memory_space=pltpu.VMEM),
        ],
        out_specs=pl.BlockSpec((9, BLOCK, columns), lambda i: (0, i, 0)),
        scratch_shapes=[pltpu.VMEM((3, window, 9 * BLOCK), jnp.bfloat16)],
        compiler_params=pltpu.CompilerParams(vmem_limit_bytes=56 * 2**20),
        cost_estimate=pl.CostEstimate(
            flops=2 * 27 * rows * window * columns,
            bytes_accessed=9 * rows * columns * 2,
            transcendentals=0,
        ),
        name="images",
    )(offs, coef, padded)


def reduce_kernel(
    scale, n_atom, n_half, f_ref, img_ref, out_ref,
    part, core_in, atom_out, atom_in, z_out, z_in,
    core_send, core_recv, atom_send, atom_recv, z_send, z_recv,
):
    me_atom = lax.axis_index("atom")
    me_mode = lax.axis_index("mode")
    core = lax.rem(me_mode, 2)
    me_z = me_mode // 2
    other = me_z * 2 + 1 - core
    own = out_ref.shape[0]
    columns = img_ref.shape[3]
    chunk = n_half * 2 * own

    barrier = pltpu.get_barrier_semaphore()
    pl.semaphore_signal(barrier, inc=1, device_id=(me_atom, other), device_id_type=MESH)
    for s in range(1, n_atom):
        to = lax.rem(me_atom + s, n_atom)
        pl.semaphore_signal(barrier, inc=1, device_id=(to, me_mode), device_id_type=MESH)
    for s in range(1, n_half):
        to = lax.rem(me_z + s, n_half) * 2 + core
        pl.semaphore_signal(barrier, inc=1, device_id=(me_atom, to), device_id_type=MESH)
    pl.semaphore_wait(barrier, n_atom + n_half - 1)

    core_copies, atom_copies = [], []

    def multiply(s):
        a_to = lax.rem(me_atom + 1 + s, n_atom)

        @pl.loop(0, 3)
        def _(q):
            total = None
            for a in range(3):
                term = lax.dot_general(
                    f_ref[a, :, pl.ds(pl.multiple_of(a_to * chunk, chunk), chunk)],
                    img_ref[q, a],
                    (((0,), (0,)), ((), ())),
                    preferred_element_type=jnp.float32,
                )
                total = term if total is None else total + term
            total = (total * scale).astype(part.dtype)
            part[s, q] = total.reshape(n_half, 2, own, columns)

        copy = pltpu.make_async_remote_copy(
            src_ref=part.at[s, :, :, 1 - core],
            dst_ref=core_in.at[s],
            send_sem=core_send.at[s],
            recv_sem=core_recv.at[s],
            device_id=(me_atom, other),
            device_id_type=MESH,
        )
        copy.start()
        core_copies.append(copy)

    def combine(s):
        core_copies[s].wait_recv()

        @pl.loop(0, n_half)
        def _(h):
            for q in range(3):
                mine = part[s, q, h, core].astype(jnp.float32)
                atom_out[s, q, h] = (mine + core_in[s, q, h].astype(jnp.float32)).astype(
                    atom_out.dtype
                )

        if s < n_atom - 1:
            a_to = lax.rem(me_atom + 1 + s, n_atom)
            copy = pltpu.make_async_remote_copy(
                src_ref=atom_out.at[s],
                dst_ref=atom_in.at[s],
                send_sem=atom_send.at[s],
                recv_sem=atom_recv.at[s],
                device_id=(a_to, me_mode),
                device_id_type=MESH,
            )
            copy.start()
            atom_copies.append(copy)

    for s in range(n_atom):
        multiply(s)
        if s >= 1:
            combine(s - 1)
    combine(n_atom - 1)

    for copy in atom_copies:
        copy.wait_recv()
    z_copies = []
    for s in range(n_half):
        h = lax.rem(me_z + 1 + s, n_half)
        for q in range(3):
            total = atom_out[n_atom - 1, q, h].astype(jnp.float32)
            for t in range(n_atom - 1):
                total = total + atom_in[t, q, h].astype(jnp.float32)
            z_out[s, q] = total.astype(z_out.dtype)
        if s < n_half - 1:
            copy = pltpu.make_async_remote_copy(
                src_ref=z_out.at[s],
                dst_ref=z_in.at[s],
                send_sem=z_send.at[s],
                recv_sem=z_recv.at[s],
                device_id=(me_atom, h * 2 + core),
                device_id_type=MESH,
            )
            copy.start()
            z_copies.append(copy)
    for copy in z_copies:
        copy.wait_recv()
    for q in range(3):
        total = z_out[n_half - 1, q].astype(jnp.float32)
        for t in range(n_half - 1):
            total = total + z_in[t, q].astype(jnp.float32)
        out_ref[:, q * columns : (q + 1) * columns] = total
    for copy in core_copies + atom_copies + z_copies:
        copy.wait_send()


def multiply_and_reduce(panel, images, scale):
    n_atom = lax.axis_size("atom")
    n_half = lax.axis_size("mode") // 2
    modes = panel.shape[2]
    columns = images.shape[2]
    rows = panel.shape[1]
    own = modes // (n_atom * n_half * 2)
    wire = jnp.bfloat16 if own % 16 == 0 else jnp.float32
    images = images.reshape(3, 3, rows, columns)
    vmem = pl.BlockSpec(memory_space=pltpu.VMEM)
    dma = pltpu.SemaphoreType.DMA
    out = pl.pallas_call(
        functools.partial(reduce_kernel, scale, n_atom, n_half),
        out_shape=jax.ShapeDtypeStruct((own, 3 * columns), jnp.float32),
        in_specs=[vmem, vmem],
        out_specs=vmem,
        scratch_shapes=[
            pltpu.VMEM((n_atom, 3, n_half, 2, own, columns), wire),
            pltpu.VMEM((n_atom, 3, n_half, own, columns), wire),
            pltpu.VMEM((n_atom, 3, n_half, own, columns), wire),
            pltpu.VMEM((n_atom - 1, 3, n_half, own, columns), wire),
            pltpu.VMEM((n_half, 3, own, columns), wire),
            pltpu.VMEM((n_half - 1, 3, own, columns), wire),
            dma((n_atom,)),
            dma((n_atom,)),
            dma((n_atom - 1,)),
            dma((n_atom - 1,)),
            dma((n_half - 1,)),
            dma((n_half - 1,)),
        ],
        compiler_params=pltpu.CompilerParams(
            collective_id=0, has_side_effects=True, vmem_limit_bytes=60 * 2**20
        ),
        cost_estimate=pl.CostEstimate(
            flops=2 * 9 * rows * modes * columns,
            bytes_accessed=9 * rows * columns * 2,
            transcendentals=0,
        ),
        name="reduce",
    )(panel, images)
    return out.reshape(own, 3, columns)


def body(first_panel, second_panel, offsets, forces, displacements):
    groups = lax.axis_size("mode")
    rows_dev = first_panel.shape[0] // groups
    atoms_all = first_panel.shape[0] * lax.axis_size("atom")
    scale = 1.0 / (3.0 * atoms_all) ** 0.5
    second_rows = lax.all_to_all(
        second_panel.transpose(1, 0, 2), "mode", split_axis=1, concat_axis=2, tiled=True
    )
    ordered, second_rows = lax.optimization_barrier((first_panel.transpose(1, 0, 2), second_rows))
    panel_rows = lax.all_to_all(ordered, "mode", split_axis=1, concat_axis=2, tiled=True)
    padded = with_rims(second_rows, RIM)
    row_start = lax.axis_index("mode") * rows_dev
    shifts = lax.dynamic_slice_in_dim(offsets, row_start, rows_dev, 1)
    force_part = lax.dynamic_slice_in_dim(forces, row_start, rows_dev, 3)
    disp_part = lax.dynamic_slice_in_dim(displacements, row_start, rows_dev, 2)
    coef = merged_blocks(shifts, force_part, disp_part)
    images = make_images(padded, shifts, coef)
    return multiply_and_reduce(panel_rows, images, scale)


def solution(mesh):
    in_specs = (
        P("atom", None, "mode"),
        P("atom", None, "mode"),
        P(None, "atom"),
        P(None, None, None, "atom"),
        P(None, None, "atom"),
    )
    out_specs = P(("atom", "mode"), None, None)
    return jax.shard_map(body, mesh=mesh, in_specs=in_specs, out_specs=out_specs, check_vma=False)
```

time: 914 us -> 423 us (0.46)
  waiting for transfers between devices: 457 us -> 163 us
  local copies, waits for them, and re-layouts: 282 us -> 48.2 us
  Pallas kernels: 0 us -> 181 us
  matrix products: 130 us -> 0 us
  between operations: 13.4 us -> 0.06 us
    unnamed x2 -> x0, waiting for transfers between devices: 288 us -> none
    gather x4 -> x0, local copies, waits for them, and re-layouts: 194 us -> none  [one_block(): gathered = padded[positions]]
    pallas_call x0 -> x2, Pallas kernels: none -> 181 us  [the longest x1 94.8 us: multiply_and_reduce(): pl.pallas_call(functools.partial(reduce_kernel, scale, n_atom, n_half), o...]
    dot_general x5 -> x0, matrix products: 130 us -> none  [the longest x4 109 us: one_block(): jnp.einsum('kqabi,kibn->iqan', blocks, gathered, preferred_element_type=j...]
    all_to_all x2, waiting for transfers between devices: 170 us -> 83.8 us  [the longest x1 83.8 us: body(): lax.all_to_all(second_panel.transpose(1, 0, 2), 'mode', split_axis=1, con...]
    ppermute x2, waiting for transfers between devices: 0.01 us -> 78.9 us  [the longest x1 78.9 us: with_rims(): low = lax.ppermute(block[:, block.shape[1] - width:], axes, forward)]
    mul x1, local copies, waits for them, and re-layouts: 18.4 us -> 0.04 us  [merged_blocks(): blocks = displacements[:, :, None, None, :] * forces[:, None, :, :, :]]
    while x1 -> x0, local copies, waits for them, and re-layouts: 14.4 us -> none  [make_images(): lax.map(one_block, jnp.arange(row_total // block_rows, dtype=jnp.int32))]
  transfers between devices with their start and end apart: 5 -> 4, of which waited for: 3 -> 2; matrix products, arithmetic and copies ran while one was open for 4% -> 8% of each run, Pallas kernels for 0% -> 20%
where the time goes in v1:
time: 423 us; the launch traced here: 422 us
  Pallas kernels  181 us (43%)
  waiting for transfers between devices  163 us (39%)
  local copies, waits for them, and re-layouts  48.2 us (11%)
  starting transfers between devices  15.1 us (4%)
  other arithmetic  14.4 us (3%)
    pallas_call x1, Pallas kernels, multiply_and_reduce(): pl.pallas_call(functools.partial(reduce_kernel, scale, n_atom, n_half), o...  94.8 us
    pallas_call x1, Pallas kernels, make_images(): pl.pallas_call(functools.partial(image_kernel, slots), grid=(rows // BLOC...  86.4 us
    all_to_all x1, waiting for transfers between devices, body(): lax.all_to_all(second_panel.transpose(1, 0, 2), 'mode', split_axis=1, con...  83.8 us
    ppermute x1, waiting for transfers between devices, with_rims(): low = lax.ppermute(block[:, block.shape[1] - width:], axes, forward)  78.9 us
    unnamed x10, local copies, waits for them, and re-layouts  13.7 us
    all_to_all x2, local copies, waits for them, and re-layouts, body(): lax.all_to_all(second_panel.transpose(1, 0, 2), 'mode', split_axis=1, con...  12.2 us
    reduce_sum x1, other arithmetic, merged_blocks(): jnp.sum(jnp.where(same[:, :, None, None, :], blocks[None], 0.0), axis=1)  9.15 us
  transfers between devices with their start and end apart: 4, of which 2 were waited for; matrix products, arithmetic and copies ran while one was open for 8% of the time, Pallas kernels for 20%

profile of v1, /device:TPU:10, one launch (start us, length us, event | category | flops | bytes accessed | tf_op | source)
XLA Modules:
  0.0 421.7 jit_solution(3630604561468072920)
XLA Ops:
  0.0 6.9 %copy.35 = bf16[4096,3,128]{2,1,0:T(4,128)(2,1)} copy(bf16[4096,3,128]{2,0,1:T(8,128)(2,1)} %param.6) | data formatting | bytes 6291456 | tf_op args[1]
  6.9 5.3 %all-to-all-start = ((bf16[3,4096,128]{2,0,1:T(4,128)(2,1)}), bf16[3,4096,128]{2,0,1:T(4,128)(2,1)}, u32[]{:S(2)}, u32[]{:S(2)}) async-start(bf16[3,4096,128]{2,0,1:T(4,128)(2,1)} %bitcast.32), calls=%async_computation | async-start | bytes 8388608 | tf_op jit(solution)/shard_map/all_to_all | solution.py:267
  12.3 6.8 %copy.36 = bf16[4096,3,128]{2,1,0:T(4,128)(2,1)} copy(bf16[4096,3,128]{2,0,1:T(8,128)(2,1)} %param.5) | data formatting | bytes 6291456 | tf_op args[0]
  19.0 83.8 %all-to-all-done = bf16[3,4096,128]{2,0,1:T(4,128)(2,1)} async-done(((bf16[3,4096,128]{2,0,1:T(4,128)(2,1)}), bf16[3,4096,128]{2,0,1:T(4,128)(2,1)}, u32[]{:S(2)}, u32[]{:S(2)}) %all-to-all-start) | async-done | bytes 3145760 | tf_op jit(solution)/shard_map/all_to_all | solution.py:267
  102.8 6.5 %copy.38 = bf16[3,8,512,128]{3,1,2,0:T(8,128)(2,1)} copy(bf16[3,8,512,128]{3,0,2,1:T(4,128)(2,1)} %bitcast.2) | data formatting | bytes 6291456 | tf_op jit(solution)/shard_map/all_to_all | solution.py:267
  109.3 5.8 %all_to_all.29 = bf16[3,512,1024]{2,1,0:T(8,128)(2,1)} reshape(bf16[3,512,8,128]{3,2,1,0:T(8,128)(2,1)} %bitcast.33) | data formatting | bytes 6291456 | tf_op jit(solution)/shard_map/all_to_all | solution.py:267
  115.0 8.0 %all-to-all-start.1 = ((bf16[3,4096,128]{2,0,1:T(4,128)(2,1)}), bf16[3,4096,128]{2,0,1:T(4,128)(2,1)}, u32[]{:S(2)}, u32[]{:S(2)}) async-start(bf16[3,4096,128]{2,0,1:T(4,128)(2,1)} %bitcast.31), calls=%async_computation.1 | async-start | bytes 8388608 | tf_op jit(solution)/shard_map/all_to_all | solution.py:271
  123.1 4.1 fusion.2
  127.2 0.1 collective-permute-start
  127.3 1.6 collective-permute-start.1
  128.9 0.9 constant_dynamic-slice_fusion.1
  129.9 0.2 fusion.1
  130.1 0.8 constant_dynamic-slice_fusion.2.offs_ref
  130.9 0.2 broadcast_compare_fusion
  131.1 9.2 %select_reduce_fusion = f32[24,9,3,512]{3,2,1,0:T(4,128)} fusion(f32[24,9,3,512]{3,0,2,1:T(8,128)S(1)} %fusion.1, pred[24,24,512]{2,1,0:T(8,128)(4,1)S(1)} %broadcast_compare_fusion), kind=kLoop, calls=%fused_computation | loop fusion | flops 15593472 | bytes 2949120 | tf_op jit(solution)/shard_map/reduce_sum | solution.py:31
  140.2 3.2 copy.27
  143.4 3.3 reshape.24.coef_ref
  146.8 78.9 %collective-permute-done = bf16[3,256,1024]{2,1,0:T(8,128)(2,1)} collective-permute-done((bf16[3,256,1024]{2,1,0:T(8,128)(2,1)}, bf16[3,256,1024]{2,1,0:T(8,128)(2,1)}, u32[]{:S(2)}, u32[]{:S(2)}) %collective-permute-start) | collective-permute-done | bytes 1572896 | tf_op jit(solution)/shard_map/ppermute | solution.py:21
  225.7 4.9 %pad_maximum_fusion.s_ref = bf16[3,1024,1024]{2,1,0:T(8,128)(2,1)} fusion(bf16[3,256,1024]{2,1,0:T(8,128)(2,1)} %collective-permute-done.1, bf16[3,512,1024]{2,1,0:T(8,128)(2,1)S(1)} %copy-done.2, bf16[3,256,1024]{2,1,0:T(8,128)(2,1)} %collective-permute-done), kind=kLoop, calls=%fused_computation.1 | loop fusion | flops 18874368 | bytes 12582912 | tf_op jit(solution)/shard_map/concatenate | solution.py:23
  230.6 86.4 %images.1 = bf16[9,512,1024]{2,1,0:T(8,128)(2,1)} custom-call(s32[24,512]{1,0:T(8,128)} %copy-done.3, f32[9,72,512]{2,1,0:T(8,128)} %reshape.24.coef_ref, bf16[3,1024,1024]{2,1,0:T(8,128)(2,1)} %pad_maximum_fusion.s_ref), custom_call_target="tpu_custom_call" | custom-call | flops 18119393280 | bytes 9437184 | tf_op jit(solution)/shard_map/images/pallas_call | solution.py:82
  317.0 4.8 %copy.37 = bf16[3,8,512,128]{3,1,2,0:T(8,128)(2,1)S(1)} copy(bf16[3,8,512,128]{3,0,2,1:T(4,128)(2,1)} %bitcast.4) | data formatting | bytes 6291456 | tf_op jit(solution)/shard_map/all_to_all | solution.py:271
  321.8 3.3 all_to_all.33.f_ref
  325.1 94.8 %reduce.1 = f32[32,3072]{1,0:T(8,128)} custom-call(bf16[3,512,1024]{2,1,0:T(8,128)(2,1)} %all_to_all.33.f_ref, bf16[3,3,512,1024]{3,2,1,0:T(8,128)(2,1)} %bitcast.38), custom_call_target="tpu_custom_call" | custom-call | flops 9663676416 | bytes 9437184 | tf_op jit(solution)/shard_map/reduce/pallas_call | solution.py:230
  419.9 1.8 copy.39
  (12 shorter events, 0.1 us)
Async XLA Ops:
  0.0 129.8 %copy-start = (f32[24,3,3,4096]{3,0,2,1:T(8,128)S(1)}, f32[24,3,3,4096]{3,0,2,1:T(8,128)}, u32[]{:S(2)}) copy-start(f32[24,3,3,4096]{3,0,2,1:T(8,128)} %param.8) | copy-start | bytes 10616836
  6.9 95.9 %all-to-all-start = ((bf16[3,4096,128]{2,0,1:T(4,128)(2,1)}), bf16[3,4096,128]{2,0,1:T(4,128)(2,1)}, u32[]{:S(2)}, u32[]{:S(2)}) async-start(bf16[3,4096,128]{2,0,1:T(4,128)(2,1)} %bitcast.32), calls=%async_computation | async-start | bytes 8388608 | tf_op jit(solution)/shard_map/all_to_all | solution.py:267
  115.0 202.0 %all-to-all-start.1 = ((bf16[3,4096,128]{2,0,1:T(4,128)(2,1)}), bf16[3,4096,128]{2,0,1:T(4,128)(2,1)}, u32[]{:S(2)}, u32[]{:S(2)}) async-start(bf16[3,4096,128]{2,0,1:T(4,128)(2,1)} %bitcast.31), calls=%async_computation.1 | async-start | bytes 8388608 | tf_op jit(solution)/shard_map/all_to_all | solution.py:271
  127.2 98.5 %collective-permute-start = (bf16[3,256,1024]{2,1,0:T(8,128)(2,1)}, bf16[3,256,1024]{2,1,0:T(8,128)(2,1)}, u32[]{:S(2)}, u32[]{:S(2)}) collective-permute-start(bf16[3,256,1024]{2,1,0:T(8,128)(2,1)} %get-tuple-element.9), channel_id=1, source_target_pairs={{0,1},{1,2},{2,3},{3,4},{4,5},{5,6},{6,7},{7,8},{8,9},{9,10},{10,1... | collective-permute-start | bytes 4718600 | tf_op jit(solution)/shard_map/ppermute | solution.py:21
  127.3 98.4 %collective-permute-start.1 = (bf16[3,256,1024]{2,1,0:T(8,128)(2,1)}, bf16[3,256,1024]{2,1,0:T(8,128)(2,1)}, u32[]{:S(2)}, u32[]{:S(2)}) collective-permute-start(bf16[3,256,1024]{2,1,0:T(8,128)(2,1)} %get-tuple-element.10), channel_id=1, source_target_pairs={{1,0},{2,1},{3,2},{4,3},{5,4},{6,5},{7,6},{8,7},{9,8},{10,9},{11,1... | collective-permute-start | bytes 4718600 | tf_op jit(solution)/shard_map/ppermute | solution.py:22
  130.9 12.5 %copy-start.3 = (s32[24,512]{1,0:T(8,128)}, s32[24,512]{1,0:T(8,128)S(1)}, u32[]{:S(2)}) copy-start(s32[24,512]{1,0:T(8,128)S(1)} %constant_dynamic-slice_fusion.2.offs_ref) | copy-start | bytes 147460
  140.2 85.5 %copy-start.2 = (bf16[3,512,1024]{2,1,0:T(8,128)(2,1)S(1)}, bf16[3,512,1024]{2,1,0:T(8,128)(2,1)}, u32[]{:S(2)}) copy-start(bf16[3,512,1024]{2,1,0:T(8,128)(2,1)} %all_to_all.29) | copy-start | bytes 9437188
  325.1 96.6 %copy-start.1 = (f32[24,3,3,4096]{3,0,2,1:T(8,128)S(1)}, f32[24,3,3,4096]{3,0,2,1:T(8,128)}, u32[]{:S(2)}) copy-start(f32[24,3,3,4096]{3,0,2,1:T(8,128)} %param.8) | copy-start | bytes 10616836

commit v2 on v1

--- a/solution.py
+++ b/solution.py
@@ -110,7 +110,7 @@
     core = lax.rem(me_mode, 2)
     me_z = me_mode // 2
     other = me_z * 2 + 1 - core
-    own = out_ref.shape[0]
+    own = out_ref.shape[1]
     columns = img_ref.shape[3]
     chunk = n_half * 2 * own
 
@@ -211,7 +211,7 @@
         total = z_out[n_half - 1, q].astype(jnp.float32)
         for t in range(n_half - 1):
             total = total + z_in[t, q].astype(jnp.float32)
-        out_ref[:, q * columns : (q + 1) * columns] = total
+        out_ref[q] = total
     for copy in core_copies + atom_copies + z_copies:
         copy.wait_send()
 
@@ -229,7 +229,7 @@
     dma = pltpu.SemaphoreType.DMA
     out = pl.pallas_call(
         functools.partial(reduce_kernel, scale, n_atom, n_half),
-        out_shape=jax.ShapeDtypeStruct((own, 3 * columns), jnp.float32),
+        out_shape=jax.ShapeDtypeStruct((3, own, columns), jnp.float32),
         in_specs=[vmem, vmem],
         out_specs=vmem,
         scratch_shapes=[
@@ -256,7 +256,7 @@
         ),
         name="reduce",
     )(panel, images)
-    return out.reshape(own, 3, columns)
+    return out.transpose(1, 0, 2)
 
 
 def body(first_panel, second_panel, offsets, forces, displacements):
@@ -267,9 +267,9 @@
     second_rows = lax.all_to_all(
         second_panel.transpose(1, 0, 2), "mode", split_axis=1, concat_axis=2, tiled=True
     )
-    ordered, second_rows = lax.optimization_barrier((first_panel.transpose(1, 0, 2), second_rows))
+    padded = with_rims(second_rows, RIM)
+    ordered, padded = lax.optimization_barrier((first_panel.transpose(1, 0, 2), padded))
     panel_rows = lax.all_to_all(ordered, "mode", split_axis=1, concat_axis=2, tiled=True)
-    padded = with_rims(second_rows, RIM)
     row_start = lax.axis_index("mode") * rows_dev
     shifts = lax.dynamic_slice_in_dim(offsets, row_start, rows_dev, 1)
     force_part = lax.dynamic_slice_in_dim(forces, row_start, rows_dev, 3)

time: 423 us -> 344 us (0.81)
  waiting for transfers between devices: 163 us -> 11.4 us
  blocking collectives: 0 us -> 96.8 us
  Pallas kernels: 181 us -> 159 us
    all_to_all x0 -> x1, blocking collectives: none -> 96.8 us  [body(): lax.all_to_all(second_panel.transpose(1, 0, 2), 'mode', split_axis=1, con...]
    all_to_all x1 -> x0, waiting for transfers between devices: 83.8 us -> none  [body(): lax.all_to_all(second_panel.transpose(1, 0, 2), 'mode', split_axis=1, con...]
    ppermute x1, waiting for transfers between devices: 78.9 us -> 9.04 us  [with_rims(): low = lax.ppermute(block[:, block.shape[1] - width:], axes, forward)]
    pallas_call x1, Pallas kernels: 94.8 us -> 72.5 us  [multiply_and_reduce(): pl.pallas_call(functools.partial(reduce_kernel, scale, n_atom, n_half), o...]
    unnamed x10 -> x13, local copies, waits for them, and re-layouts: 13.7 us -> 27.8 us
    all_to_all x1 -> x0, starting transfers between devices: 5.32 us -> none  [body(): lax.all_to_all(second_panel.transpose(1, 0, 2), 'mode', split_axis=1, con...]
  transfers between devices with their start and end apart: 4 -> 3, of which waited for: 2 -> 2; matrix products, arithmetic and copies ran while one was open for 8% -> 9% of each run, Pallas kernels for 20% -> 25%
where the time goes in v2:
time: 344 us
  Pallas kernels  159 us (46%)
  blocking collectives  96.8 us (28%)
  local copies, waits for them, and re-layouts  52.3 us (15%)
  starting transfers between devices  13.2 us (4%)
  waiting for transfers between devices  11.4 us (3%)
  other arithmetic  11.2 us (3%)
    all_to_all x1, blocking collectives, body(): lax.all_to_all(second_panel.transpose(1, 0, 2), 'mode', split_axis=1, con...  96.8 us
    pallas_call x1, Pallas kernels, make_images(): pl.pallas_call(functools.partial(image_kernel, slots), grid=(rows // BLOC...  86.4 us
    pallas_call x1, Pallas kernels, multiply_and_reduce(): pl.pallas_call(functools.partial(reduce_kernel, scale, n_atom, n_half), o...  72.5 us
    unnamed x13, local copies, waits for them, and re-layouts  27.8 us
    all_to_all x1, starting transfers between devices, body(): lax.all_to_all(ordered, 'mode', split_axis=1, concat_axis=2, tiled=True)  11.5 us
    all_to_all x2, local copies, waits for them, and re-layouts, body(): lax.all_to_all(second_panel.transpose(1, 0, 2), 'mode', split_axis=1, con...  10.1 us
    ppermute x1, waiting for transfers between devices, with_rims(): low = lax.ppermute(block[:, block.shape[1] - width:], axes, forward)  9.04 us
    all_to_all x2, local copies, waits for them, and re-layouts, body(): lax.all_to_all(ordered, 'mode', split_axis=1, concat_axis=2, tiled=True)  8.1 us
  transfers between devices with their start and end apart: 3, of which 2 were waited for; matrix products, arithmetic and copies ran while one was open for 9% of the time, Pallas kernels for 25%

profile of v2, /device:TPU:10, one launch (start us, length us, event | category | flops | bytes accessed | tf_op | source)
XLA Modules:
  0.0 343.9 jit_solution(15209111706040439656)
XLA Ops:
  0.0 5.5 %copy.29 = bf16[4096,3,128]{2,1,0:T(4,128)(2,1)S(1)} copy(bf16[4096,3,128]{2,0,1:T(8,128)(2,1)} %param.6) | data formatting | bytes 6291456 | tf_op args[1]
  5.5 96.8 %all_to_all.36 = bf16[3,4096,128]{2,0,1:T(4,128)(2,1)S(1)} all-to-all(bf16[3,4096,128]{2,0,1:T(4,128)(2,1)S(1)} %bitcast.30), channel_id=1, replica_groups=mesh['atom'=4,'mode'=8] {'mode'}, dimensions={1} | all-to-all | bytes 6291456 | tf_op jit(solution)/shard_map/all_to_all | solution.py:267
  102.3 4.2 %copy.32 = bf16[3,8,512,128]{3,1,2,0:T(8,128)(2,1)} copy(bf16[3,8,512,128]{3,0,2,1:T(4,128)(2,1)S(1)} %bitcast.29) | data formatting | bytes 6291456 | tf_op jit(solution)/shard_map/all_to_all | solution.py:267
  106.5 5.8 %all_to_all.29 = bf16[3,512,1024]{2,1,0:T(8,128)(2,1)} reshape(bf16[3,512,8,128]{3,2,1,0:T(8,128)(2,1)} %bitcast.31) | data formatting | bytes 6291456 | tf_op jit(solution)/shard_map/all_to_all | solution.py:267
  112.4 2.4 fusion.2
  114.8 0.1 collective-permute-start
  114.9 1.7 collective-permute-start.1
  116.6 20.4 %copy.30 = bf16[4096,3,128]{2,1,0:T(4,128)(2,1)} copy(bf16[4096,3,128]{2,0,1:T(8,128)(2,1)S(1)} %copy-done.3) | data formatting | bytes 6291456 | tf_op args[0]
  137.0 9.0 %collective-permute-done = bf16[3,256,1024]{2,1,0:T(8,128)(2,1)S(1)} collective-permute-done((bf16[3,256,1024]{2,1,0:T(8,128)(2,1)S(1)}, bf16[3,256,1024]{2,1,0:T(8,128)(2,1)S(1)}, u32[]{:S(2)}, u32[]{:S(2)}) %collective-permute-start) | collective-permute-done | bytes 1572896 | tf_op jit(solution)/shard_map/ppermute | solution.py:21
  146.1 2.3 collective-permute-done.1
  148.4 3.0 pad_maximum_fusion.s_ref
  151.4 11.5 %all-to-all-start.1 = ((bf16[3,4096,128]{2,0,1:T(4,128)(2,1)}), bf16[3,4096,128]{2,0,1:T(4,128)(2,1)}, u32[]{:S(2)}, u32[]{:S(2)}) async-start(bf16[3,4096,128]{2,0,1:T(4,128)(2,1)} %bitcast.28), calls=%async_computation.1 | async-start | bytes 8388608 | tf_op jit(solution)/shard_map/all_to_all | solution.py:272
  162.8 0.9 constant_dynamic-slice_fusion.1
  163.9 0.2 fusion.1
  164.0 0.8 constant_dynamic-slice_fusion.2.offs_ref
  164.8 0.2 broadcast_compare_fusion
  165.0 7.9 %select_reduce_fusion = f32[24,9,3,512]{3,2,1,0:T(4,128)S(1)} fusion(f32[24,9,3,512]{3,0,2,1:T(8,128)S(1)} %fusion.1, pred[24,24,512]{2,1,0:T(8,128)(4,1)S(1)} %broadcast_compare_fusion), kind=kLoop, calls=%fused_computation | loop fusion | flops 15593472 | bytes 2949120 | tf_op jit(solution)/shard_map/reduce_sum | solution.py:31
  172.9 0.4 copy.24
  173.3 1.8 reshape.21.coef_ref
  175.1 86.4 %images.1 = bf16[9,512,1024]{2,1,0:T(8,128)(2,1)} custom-call(s32[24,512]{1,0:T(8,128)} %copy-done.4, f32[9,72,512]{2,1,0:T(8,128)} %reshape.21.coef_ref, bf16[3,1024,1024]{2,1,0:T(8,128)(2,1)} %pad_maximum_fusion.s_ref), custom_call_target="tpu_custom_call" | custom-call | flops 18119393280 | bytes 9437184 | tf_op jit(solution)/shard_map/images/pallas_call | solution.py:82
  261.5 4.8 %copy.31 = bf16[3,8,512,128]{3,1,2,0:T(8,128)(2,1)S(1)} copy(bf16[3,8,512,128]{3,0,2,1:T(4,128)(2,1)} %bitcast.4) | data formatting | bytes 6291456 | tf_op jit(solution)/shard_map/all_to_all | solution.py:272
  266.3 3.3 all_to_all.33.f_ref
  269.6 72.5 %reduce.1 = f32[3,32,1024]{2,1,0:T(8,128)} custom-call(bf16[3,512,1024]{2,1,0:T(8,128)(2,1)} %all_to_all.33.f_ref, bf16[3,3,512,1024]{3,2,1,0:T(8,128)(2,1)} %bitcast.36), custom_call_target="tpu_custom_call" | custom-call | flops 9663676416 | bytes 9437184 | tf_op jit(solution)/shard_map/reduce/pallas_call | solution.py:230
  342.1 1.8 copy.34
  (13 shorter events, 0.1 us)
Async XLA Ops:
  0.0 163.7 %copy-start = (f32[24,3,3,4096]{3,0,2,1:T(8,128)S(1)}, f32[24,3,3,4096]{3,0,2,1:T(8,128)}, u32[]{:S(2)}) copy-start(f32[24,3,3,4096]{3,0,2,1:T(8,128)} %param.8) | copy-start | bytes 10616836
  112.4 4.2 %copy-start.3 = (bf16[4096,3,128]{2,0,1:T(8,128)(2,1)S(1)}, bf16[4096,3,128]{2,0,1:T(8,128)(2,1)}, u32[]{:S(2)}) copy-start(bf16[4096,3,128]{2,0,1:T(8,128)(2,1)} %param.5) | copy-start | bytes 9437188
  114.8 31.3 %collective-permute-start = (bf16[3,256,1024]{2,1,0:T(8,128)(2,1)S(1)}, bf16[3,256,1024]{2,1,0:T(8,128)(2,1)S(1)}, u32[]{:S(2)}, u32[]{:S(2)}) collective-permute-start(bf16[3,256,1024]{2,1,0:T(8,128)(2,1)S(1)} %get-tuple-element.9), channel_id=1, source_target_pairs={{0,1},{1,2},{2,3},{3,4},{4,5},{5,6},{6,7},{7,8},{8,9},{9,10},{10,1... | collective-permute-start | bytes 4718600 | tf_op jit(solution)/shard_map/ppermute | solution.py:21
  114.8 33.6 %copy-start.2 = (bf16[3,512,1024]{2,1,0:T(8,128)(2,1)S(1)}, bf16[3,512,1024]{2,1,0:T(8,128)(2,1)}, u32[]{:S(2)}) copy-start(bf16[3,512,1024]{2,1,0:T(8,128)(2,1)} %all_to_all.29) | copy-start | bytes 9437188
  114.9 33.5 %collective-permute-start.1 = (bf16[3,256,1024]{2,1,0:T(8,128)(2,1)S(1)}, bf16[3,256,1024]{2,1,0:T(8,128)(2,1)S(1)}, u32[]{:S(2)}, u32[]{:S(2)}) collective-permute-start(bf16[3,256,1024]{2,1,0:T(8,128)(2,1)S(1)} %get-tuple-element.10), channel_id=1, source_target_pairs={{1,0},{2,1},{3,2},{4,3},{5,4},{6,5},{7,6},{8,7},{9,8},{10,9},{11,1... | collective-permute-start | bytes 4718600 | tf_op jit(solution)/shard_map/ppermute | solution.py:22
  151.4 110.1 %all-to-all-start.1 = ((bf16[3,4096,128]{2,0,1:T(4,128)(2,1)}), bf16[3,4096,128]{2,0,1:T(4,128)(2,1)}, u32[]{:S(2)}, u32[]{:S(2)}) async-start(bf16[3,4096,128]{2,0,1:T(4,128)(2,1)} %bitcast.28), calls=%async_computation.1 | async-start | bytes 8388608 | tf_op jit(solution)/shard_map/all_to_all | solution.py:272
  164.8 8.1 %copy-start.4 = (s32[24,512]{1,0:T(8,128)}, s32[24,512]{1,0:T(8,128)S(1)}, u32[]{:S(2)}) copy-start(s32[24,512]{1,0:T(8,128)S(1)} %constant_dynamic-slice_fusion.2.offs_ref) | copy-start | bytes 147460
  269.6 74.2 %copy-start.1 = (f32[24,3,3,4096]{3,0,2,1:T(8,128)S(1)}, f32[24,3,3,4096]{3,0,2,1:T(8,128)}, u32[]{:S(2)}) copy-start(f32[24,3,3,4096]{3,0,2,1:T(8,128)} %param.8) | copy-start | bytes 10616836

commit v3 on v2

--- a/solution.py
+++ b/solution.py
@@ -21,6 +21,89 @@
     low = lax.ppermute(block[:, block.shape[1] - width :], axes, forward)
     high = lax.ppermute(block[:, :width], axes, backward)
     return jnp.concatenate([low, block, high], axis=1)
+
+
+def exchange_kernel(
+    n_atom, groups, s_ref, out_ref, send, recv, rim_send, rim_recv, local
+):
+    me_atom = lax.axis_index("atom")
+    me = lax.axis_index("mode")
+    width = s_ref.shape[2]
+    rows = s_ref.shape[1] // groups
+    number = me_atom * groups + me
+    count = n_atom * groups
+    after = lax.rem(number + 1, count)
+    before = lax.rem(number + count - 1, count)
+    after = (after // groups, lax.rem(after, groups))
+    before = (before // groups, lax.rem(before, groups))
+
+    barrier = pltpu.get_barrier_semaphore()
+    for s in range(1, groups):
+        to = lax.rem(me + s, groups)
+        pl.semaphore_signal(barrier, inc=1, device_id=(me_atom, to), device_id_type=MESH)
+    pl.semaphore_signal(barrier, inc=1, device_id=after, device_id_type=MESH)
+    pl.semaphore_signal(barrier, inc=1, device_id=before, device_id_type=MESH)
+    pl.semaphore_wait(barrier, groups + 1)
+
+    columns = pl.ds(pl.multiple_of(me * width, width), width)
+    landing = out_ref.at[:, pl.ds(RIM, rows), columns]
+    copies = []
+    for s in range(1, groups):
+        to = lax.rem(me + s, groups)
+        copy = pltpu.make_async_remote_copy(
+            src_ref=s_ref.at[:, pl.ds(pl.multiple_of(to * rows, rows), rows), :],
+            dst_ref=landing,
+            send_sem=send.at[s - 1],
+            recv_sem=recv.at[s - 1],
+            device_id=(me_atom, to),
+            device_id_type=MESH,
+        )
+        copy.start()
+        copies.append(copy)
+    mine = pltpu.make_async_copy(
+        s_ref.at[:, pl.ds(pl.multiple_of(me * rows, rows), rows), :], landing, local
+    )
+    mine.start()
+    mine.wait()
+    for copy in copies:
+        copy.wait_recv()
+
+    rims = []
+    for at, (source, target, device) in enumerate(
+        ((rows, 0, after), (RIM, RIM + rows, before))
+    ):
+        copy = pltpu.make_async_remote_copy(
+            src_ref=out_ref.at[:, pl.ds(source, RIM), :],
+            dst_ref=out_ref.at[:, pl.ds(target, RIM), :],
+            send_sem=rim_send.at[at],
+            recv_sem=rim_recv.at[at],
+            device_id=device,
+            device_id_type=MESH,
+        )
+        copy.start()
+        rims.append(copy)
+    for copy in rims:
+        copy.wait_recv()
+    for copy in copies + rims:
+        copy.wait_send()
+
+
+def exchange_with_rims(panel):
+    n_atom, groups = lax.axis_size("atom"), lax.axis_size("mode")
+    rows, width = panel.shape[1] // groups, panel.shape[2]
+    if width % 128:
+        whole = lax.all_to_all(panel, "mode", split_axis=1, concat_axis=2, tiled=True)
+        return with_rims(whole, RIM)
+    dma = pltpu.SemaphoreType.DMA
+    return pl.pallas_call(
+        functools.partial(exchange_kernel, n_atom, groups),
+        out_shape=jax.ShapeDtypeStruct((3, rows + 2 * RIM, width * groups), panel.dtype),
+        in_specs=[pl.BlockSpec(memory_space=pl.ANY)],
+        out_specs=pl.BlockSpec(memory_space=pl.ANY),
+        scratch_shapes=[dma((groups - 1,)), dma((groups - 1,)), dma((2,)), dma((2,)), dma],
+        compiler_params=pltpu.CompilerParams(collective_id=1, has_side_effects=True),
+        name="exchange",
+    )(panel)
 
 
 def merged_blocks(offsets, forces, displacements):
@@ -264,10 +347,7 @@
     rows_dev = first_panel.shape[0] // groups
     atoms_all = first_panel.shape[0] * lax.axis_size("atom")
     scale = 1.0 / (3.0 * atoms_all) ** 0.5
-    second_rows = lax.all_to_all(
-        second_panel.transpose(1, 0, 2), "mode", split_axis=1, concat_axis=2, tiled=True
-    )
-    padded = with_rims(second_rows, RIM)
+    padded = exchange_with_rims(second_panel.transpose(1, 0, 2))
     ordered, padded = lax.optimization_barrier((first_panel.transpose(1, 0, 2), padded))
     panel_rows = lax.all_to_all(ordered, "mode", split_axis=1, concat_axis=2, tiled=True)
     row_start = lax.axis_index("mode") * rows_dev

time: 344 us -> 318 us (0.924)
  blocking collectives: 96.8 us -> 0 us
  Pallas kernels: 159 us -> 248 us
  local copies, waits for them, and re-layouts: 52.3 us -> 29.8 us
  starting transfers between devices: 13.2 us -> 28.2 us
  waiting for transfers between devices: 11.4 us -> 0.01 us
    all_to_all x1 -> x0, blocking collectives: 96.8 us -> none  [body(): lax.all_to_all(second_panel.transpose(1, 0, 2), 'mode', split_axis=1, con...]
    pallas_call x0 -> x1, Pallas kernels: none -> 89.9 us  [exchange_with_rims(): pl.pallas_call(functools.partial(exchange_kernel, n_atom, groups), out_sh...]
    unnamed x13 -> x6, local copies, waits for them, and re-layouts: 27.8 us -> 9.3 us
    all_to_all x1, starting transfers between devices: 11.5 us -> 28.2 us  [body(): lax.all_to_all(ordered, 'mode', split_axis=1, concat_axis=2, tiled=True)]
    ppermute x2 -> x0, waiting for transfers between devices: 11.4 us -> none  [the longest x1 9.04 us: with_rims(): low = lax.ppermute(block[:, block.shape[1] - width:], axes, forward)]
    all_to_all x2 -> x0, local copies, waits for them, and re-layouts: 10.1 us -> none  [body(): lax.all_to_all(second_panel.transpose(1, 0, 2), 'mode', split_axis=1, con...]
    all_to_all x2, local copies, waits for them, and re-layouts: 8.1 us -> 12.2 us  [body(): lax.all_to_all(ordered, 'mode', split_axis=1, concat_axis=2, tiled=True)]
  transfers between devices with their start and end apart: 3 -> 1, of which waited for: 2 -> 0; matrix products, arithmetic and copies ran while one was open for 9% -> 6% of each run, Pallas kernels for 25% -> 27%
where the time goes in v3:
time: 318 us; the launch traced here: 317 us
  Pallas kernels  248 us (78%)
  local copies, waits for them, and re-layouts  29.8 us (9%)
  starting transfers between devices  28.2 us (9%)
  other arithmetic  11.2 us (4%)
    pallas_call x1, Pallas kernels, exchange_with_rims(): pl.pallas_call(functools.partial(exchange_kernel, n_atom, groups), out_sh...  89.9 us
    pallas_call x1, Pallas kernels, make_images(): pl.pallas_call(functools.partial(image_kernel, slots), grid=(rows // BLOC...  86.4 us
    pallas_call x1, Pallas kernels, multiply_and_reduce(): pl.pallas_call(functools.partial(reduce_kernel, scale, n_atom, n_half), o...  71.8 us
    all_to_all x1, starting transfers between devices, body(): lax.all_to_all(ordered, 'mode', split_axis=1, concat_axis=2, tiled=True)  28.2 us
    all_to_all x2, local copies, waits for them, and re-layouts, body(): lax.all_to_all(ordered, 'mode', split_axis=1, concat_axis=2, tiled=True)  12.2 us
    reduce_sum x1, other arithmetic, merged_blocks(): jnp.sum(jnp.where(same[:, :, None, None, :], blocks[None], 0.0), axis=1)  10.1 us
    unnamed x6, local copies, waits for them, and re-layouts  9.3 us
  transfers between devices with their start and end apart: 1, of which 0 were waited for; matrix products, arithmetic and copies ran while one was open for 6% of the time, Pallas kernels for 27%

profile of v3, /device:TPU:10, one launch (start us, length us, event | category | flops | bytes accessed | tf_op | source)
XLA Modules:
  0.0 317.2 jit_solution(18192673489127708667)
XLA Ops:
  0.0 0.0 copy-start
  0.0 6.9 %copy.21 = bf16[4096,3,128]{2,1,0:T(4,128)(2,1)} copy(bf16[4096,3,128]{2,0,1:T(8,128)(2,1)} %param.5) | data formatting | bytes 6291456 | tf_op args[0]
  6.9 89.9 %exchange.1.s_ref = bf16[3,1024,1024]{2,1,0:T(8,128)(2,1)} custom-call(bf16[3,4096,128]{2,1,0:T(8,128)(2,1)} %bitcast.23), custom_call_target="tpu_custom_call" | custom-call | tf_op jit(solution)/shard_map/exchange/pallas_call | solution.py:98
  96.8 28.2 %all-to-all-start = ((bf16[3,4096,128]{2,0,1:T(4,128)(2,1)}), bf16[3,4096,128]{2,0,1:T(4,128)(2,1)}, u32[]{:S(2)}, u32[]{:S(2)}) async-start(bf16[3,4096,128]{2,0,1:T(4,128)(2,1)} %bitcast.20), calls=%async_computation | async-start | bytes 8388608 | tf_op jit(solution)/shard_map/all_to_all | solution.py:352
  125.0 0.9 constant_dynamic-slice_fusion.1
  125.9 0.0 copy-done
  126.0 0.2 fusion.1
  126.2 0.8 constant_dynamic-slice_fusion.2.offs_ref
  127.0 0.0 copy-start.1
  127.0 0.6 copy-done.1
  127.6 0.9 broadcast_compare_fusion
  128.5 10.1 %select_reduce_fusion = f32[24,9,3,512]{3,2,1,0:T(4,128)} fusion(f32[24,9,3,512]{3,0,2,1:T(8,128)S(1)} %fusion.1, pred[24,24,512]{2,1,0:T(8,128)(4,1)} %broadcast_compare_fusion), kind=kLoop, calls=%fused_computation | loop fusion | flops 15593472 | bytes 2949120 | tf_op jit(solution)/shard_map/reduce_sum | solution.py:114
  138.6 3.1 copy.18
  141.7 3.3 %reshape.21.coef_ref = f32[9,72,512]{2,1,0:T(8,128)} reshape(f32[9,24,3,512]{3,2,1,0:T(4,128)} %copy.18) | data formatting | bytes 2654208 | tf_op jit(solution)/shard_map/reshape | solution.py:117
  145.0 86.4 %images.1 = bf16[9,512,1024]{2,1,0:T(8,128)(2,1)} custom-call(s32[24,512]{1,0:T(8,128)} %copy-done.1, f32[9,72,512]{2,1,0:T(8,128)} %reshape.21.coef_ref, bf16[3,1024,1024]{2,1,0:T(8,128)(2,1)} %exchange.1.s_ref), custom_call_target="tpu_custom_call" | custom-call | flops 18119393280 | bytes 9437184 | tf_op jit(solution)/shard_map/images/pallas_call | solution.py:165
  231.4 0.0 all-to-all-done
  231.4 6.4 %copy.22 = bf16[3,8,512,128]{3,1,2,0:T(8,128)(2,1)} copy(bf16[3,8,512,128]{3,0,2,1:T(4,128)(2,1)} %bitcast.2) | data formatting | bytes 6291456 | tf_op jit(solution)/shard_map/all_to_all | solution.py:352
  237.8 5.8 %all_to_all.16.f_ref = bf16[3,512,1024]{2,1,0:T(8,128)(2,1)} reshape(bf16[3,512,8,128]{3,2,1,0:T(8,128)(2,1)} %bitcast.21) | data formatting | bytes 6291456 | tf_op jit(solution)/shard_map/all_to_all | solution.py:352
  243.6 71.8 %reduce.1 = f32[3,32,1024]{2,1,0:T(8,128)} custom-call(bf16[3,512,1024]{2,1,0:T(8,128)(2,1)} %all_to_all.16.f_ref, bf16[3,3,512,1024]{3,2,1,0:T(8,128)(2,1)} %bitcast.26), custom_call_target="tpu_custom_call" | custom-call | flops 9663676416 | bytes 9437184 | tf_op jit(solution)/shard_map/reduce/pallas_call | solution.py:313
  315.5 1.8 copy.24
  (2 shorter events, 0.1 us)
Async XLA Ops:
  0.0 125.9 %copy-start = (f32[24,3,3,4096]{3,0,2,1:T(8,128)S(1)}, f32[24,3,3,4096]{3,0,2,1:T(8,128)}, u32[]{:S(2)}) copy-start(f32[24,3,3,4096]{3,0,2,1:T(8,128)} %param.8) | copy-start | bytes 10616836
  96.8 134.6 %all-to-all-start = ((bf16[3,4096,128]{2,0,1:T(4,128)(2,1)}), bf16[3,4096,128]{2,0,1:T(4,128)(2,1)}, u32[]{:S(2)}, u32[]{:S(2)}) async-start(bf16[3,4096,128]{2,0,1:T(4,128)(2,1)} %bitcast.20), calls=%async_computation | async-start | bytes 8388608 | tf_op jit(solution)/shard_map/all_to_all | solution.py:352
  127.0 0.6 copy-start.1

commit v4 on v3

--- a/solution.py
+++ b/solution.py
@@ -115,6 +115,95 @@
         jnp.where(same[:, :, None, None, :], blocks[None], 0.0), axis=1
     )
     return merged.transpose(1, 0, 2, 3).reshape(9, slots * 3, rows)
+
+
+def panel_copies(groups, f_ref, panel_ref, send, recv, local):
+    me_atom = lax.axis_index("atom")
+    me = lax.axis_index("mode")
+    width = f_ref.shape[2]
+    rows = panel_ref.shape[1]
+    landing = panel_ref.at[:, :, pl.ds(pl.multiple_of(me * width, width), width)]
+    mine = pltpu.make_async_copy(
+        f_ref.at[:, pl.ds(pl.multiple_of(me * rows, rows), rows), :], landing, local
+    )
+    copies = []
+    for s in range(1, groups):
+        to = lax.rem(me + s, groups)
+        copies.append(
+            pltpu.make_async_remote_copy(
+                src_ref=f_ref.at[:, pl.ds(pl.multiple_of(to * rows, rows), rows), :],
+                dst_ref=landing,
+                send_sem=send.at[s - 1],
+                recv_sem=recv.at[s - 1],
+                device_id=(me_atom, to),
+                device_id_type=MESH,
+            )
+        )
+    return mine, copies
+
+
+def image_panel_kernel(
+    slots, groups, offs_ref, coef_ref, s_ref, f_ref, out_ref, panel_ref, w_ref, send, recv, local
+):
+    @pl.when(pl.program_id(0) == 0)
+    def _():
+        me_atom = lax.axis_index("atom")
+        me = lax.axis_index("mode")
+        barrier = pltpu.get_barrier_semaphore()
+        for s in range(1, groups):
+            to = lax.rem(me + s, groups)
+            pl.semaphore_signal(barrier, inc=1, device_id=(me_atom, to), device_id_type=MESH)
+        pl.semaphore_wait(barrier, groups - 1)
+        mine, copies = panel_copies(groups, f_ref, panel_ref, send, recv, local)
+        for copy in copies:
+            copy.start()
+        mine.start()
+
+    image_kernel(slots, offs_ref, coef_ref, s_ref, out_ref, w_ref)
+
+    @pl.when(pl.program_id(0) == pl.num_programs(0) - 1)
+    def _():
+        mine, copies = panel_copies(groups, f_ref, panel_ref, send, recv, local)
+        mine.wait()
+        for copy in copies:
+            copy.wait()
+
+
+def make_images_and_panel(padded, offs, coef, panel):
+    slots, rows = offs.shape
+    columns = padded.shape[2]
+    window = BLOCK + 2 * RIM
+    groups = lax.axis_size("mode")
+    width = panel.shape[2]
+    dma = pltpu.SemaphoreType.DMA
+    return pl.pallas_call(
+        functools.partial(image_panel_kernel, slots, groups),
+        grid=(rows // BLOCK,),
+        out_shape=(
+            jax.ShapeDtypeStruct((9, rows, columns), jnp.bfloat16),
+            jax.ShapeDtypeStruct((3, rows, groups * width), panel.dtype),
+        ),
+        in_specs=[
+            pl.BlockSpec((slots, BLOCK), lambda i: (0, i)),
+            pl.BlockSpec((9, slots * 3, BLOCK), lambda i: (0, 0, i)),
+            pl.BlockSpec(memory_space=pltpu.VMEM),
+            pl.BlockSpec(memory_space=pl.ANY),
+        ],
+        out_specs=(
+            pl.BlockSpec((9, BLOCK, columns), lambda i: (0, i, 0)),
+            pl.BlockSpec(memory_space=pl.ANY),
+        ),
+        scratch_shapes=[
+            pltpu.VMEM((3, window, 9 * BLOCK), jnp.bfloat16),
+            dma((groups - 1,)),
+            dma((groups - 1,)),
+            dma,
+        ],
+        compiler_params=pltpu.CompilerParams(
+            collective_id=2, has_side_effects=True, vmem_limit_bytes=56 * 2**20
+        ),
+        name="images_panel",
+    )(offs, coef, padded, panel)
 
 
 def image_kernel(slots, offs_ref, coef_ref, s_ref, out_ref, w_ref):
@@ -348,14 +437,18 @@
     atoms_all = first_panel.shape[0] * lax.axis_size("atom")
     scale = 1.0 / (3.0 * atoms_all) ** 0.5
     padded = exchange_with_rims(second_panel.transpose(1, 0, 2))
-    ordered, padded = lax.optimization_barrier((first_panel.transpose(1, 0, 2), padded))
-    panel_rows = lax.all_to_all(ordered, "mode", split_axis=1, concat_axis=2, tiled=True)
     row_start = lax.axis_index("mode") * rows_dev
     shifts = lax.dynamic_slice_in_dim(offsets, row_start, rows_dev, 1)
     force_part = lax.dynamic_slice_in_dim(forces, row_start, rows_dev, 3)
     disp_part = lax.dynamic_slice_in_dim(displacements, row_start, rows_dev, 2)
     coef = merged_blocks(shifts, force_part, disp_part)
-    images = make_images(padded, shifts, coef)
+    ordered = first_panel.transpose(1, 0, 2)
+    if ordered.shape[2] % 128:
+        ordered, padded = lax.optimization_barrier((ordered, padded))
+        panel_rows = lax.all_to_all(ordered, "mode", split_axis=1, concat_axis=2, tiled=True)
+        images = make_images(padded, shifts, coef)
+    else:
+        images, panel_rows = make_images_and_panel(padded, shifts, coef, ordered)
     return multiply_and_reduce(panel_rows, images, scale)
 
 

time: 318 us -> 294 us (0.925)
  starting transfers between devices: 28.2 us -> 0 us
  Pallas kernels: 248 us -> 272 us
  local copies, waits for them, and re-layouts: 29.8 us -> 10.3 us
    all_to_all x1 -> x0, starting transfers between devices: 28.2 us -> none  [body(): lax.all_to_all(ordered, 'mode', split_axis=1, concat_axis=2, tiled=True)]
    pallas_call x1, Pallas kernels: 86.4 us -> 111 us  [make_images_and_panel(): pl.pallas_call(functools.partial(image_panel_kernel, slots, groups), grid...]
    all_to_all x2 -> x0, local copies, waits for them, and re-layouts: 12.2 us -> none  [body(): lax.all_to_all(ordered, 'mode', split_axis=1, concat_axis=2, tiled=True)]
    unnamed x6 -> x5, local copies, waits for them, and re-layouts: 9.3 us -> 1.78 us
  transfers between devices with their start and end apart: 1 -> 0, of which waited for: 0 -> 0; matrix products, arithmetic and copies ran while one was open for 6% -> 0% of each run, Pallas kernels for 27% -> 0%
where the time goes in v4:
time: 294 us
  Pallas kernels  272 us (93%)
  other arithmetic  11.2 us (4%)
  local copies, waits for them, and re-layouts  10.3 us (4%)
    pallas_call x1, Pallas kernels, make_images_and_panel(): pl.pallas_call(functools.partial(image_panel_kernel, slots, groups), grid...  111 us
    pallas_call x1, Pallas kernels, exchange_with_rims(): pl.pallas_call(functools.partial(exchange_kernel, n_atom, groups), out_sh...  89.9 us
    pallas_call x1, Pallas kernels, multiply_and_reduce(): pl.pallas_call(functools.partial(reduce_kernel, scale, n_atom, n_half), o...  71.8 us
    reduce_sum x1, other arithmetic, merged_blocks(): jnp.sum(jnp.where(same[:, :, None, None, :], blocks[None], 0.0), axis=1)  10.1 us

profile of v4, /device:TPU:10, one launch (start us, length us, event | category | flops | bytes accessed | tf_op | source)
XLA Modules:
  0.0 293.7 jit_solution(15141498901495052512)
XLA Ops:
  0.0 0.0 copy-start
  0.0 1.0 constant_dynamic-slice_fusion.2.offs_ref
  1.0 0.0 copy-start.1
  1.0 1.1 constant_dynamic-slice_fusion.1
  2.1 0.9 broadcast_compare_fusion
  3.0 0.0 copy-done.1
  3.0 0.0 copy-done
  3.0 0.2 fusion.1
  3.2 10.1 %select_reduce_fusion = f32[24,9,3,512]{3,2,1,0:T(4,128)} fusion(f32[24,9,3,512]{3,0,2,1:T(8,128)S(1)} %fusion.1, pred[24,24,512]{2,1,0:T(8,128)(4,1)} %broadcast_compare_fusion), kind=kLoop, calls=%fused_computation | loop fusion | flops 15593472 | bytes 2949120 | tf_op jit(solution)/shard_map/reduce_sum | solution.py:114
  13.3 3.1 %copy.10 = f32[9,24,3,512]{3,2,1,0:T(4,128)} copy(f32[9,24,3,512]{3,2,0,1:T(4,128)} %bitcast.12) | data formatting | bytes 2654208 | tf_op jit(solution)/shard_map/transpose | solution.py:117
  16.4 3.3 %reshape.21.coef_ref = f32[9,72,512]{2,1,0:T(8,128)} reshape(f32[9,24,3,512]{3,2,1,0:T(4,128)} %copy.10) | data formatting | bytes 2654208 | tf_op jit(solution)/shard_map/reshape | solution.py:117
  19.7 89.9 %exchange.1.s_ref = bf16[3,1024,1024]{2,1,0:T(8,128)(2,1)} custom-call(bf16[3,4096,128]{2,1,0:T(8,128)(2,1)} %bitcast.13), custom_call_target="tpu_custom_call" | custom-call | tf_op jit(solution)/shard_map/exchange/pallas_call | solution.py:98
  109.6 110.5 %images_panel.1 = (bf16[9,512,1024]{2,1,0:T(8,128)(2,1)}, bf16[3,512,1024]{2,1,0:T(8,128)(2,1)}) custom-call(s32[24,512]{1,0:T(8,128)} %copy-done.1, f32[9,72,512]{2,1,0:T(8,128)} %reshape.21.coef_ref, bf16[3,1024,1024]{2,1,0:T(8,128)(2,1)} %exchange.1.s_ref, bf16[3,4096,128]{2,1,0:T(8,128)(2,1)} %bitcast.14), custom_call_target="tpu_custom_call" | custom-call | tf_op jit(solution)/shard_map/images_panel/pallas_call | solution.py:179
  220.1 71.8 %reduce.1 = f32[3,32,1024]{2,1,0:T(8,128)} custom-call(bf16[3,512,1024]{2,1,0:T(8,128)(2,1)} %get-tuple-element.7.f_ref, bf16[3,3,512,1024]{3,2,1,0:T(8,128)(2,1)} %bitcast.17), custom_call_target="tpu_custom_call" | custom-call | flops 9663676416 | bytes 9437184 | tf_op jit(solution)/shard_map/reduce/pallas_call | solution.py:402
  291.9 1.8 copy.12
  (2 shorter events, 0.1 us)
Async XLA Ops:
  0.0 3.0 %copy-start = (f32[24,3,3,4096]{3,0,2,1:T(8,128)S(1)}, f32[24,3,3,4096]{3,0,2,1:T(8,128)}, u32[]{:S(2)}) copy-start(f32[24,3,3,4096]{3,0,2,1:T(8,128)} %param.8) | copy-start | bytes 10616836
  1.0 2.0 copy-start.1

commit v5 on v4

--- a/solution.py
+++ b/solution.py
@@ -24,7 +24,8 @@
 
 
 def exchange_kernel(
-    n_atom, groups, s_ref, out_ref, send, recv, rim_send, rim_recv, local
+    n_atom, groups, s_ref, offs_ref, block_ref, out_ref, coef_ref,
+    send, recv, rim_send, rim_recv, local,
 ):
     me_atom = lax.axis_index("atom")
     me = lax.axis_index("mode")
@@ -64,6 +65,19 @@
         s_ref.at[:, pl.ds(pl.multiple_of(me * rows, rows), rows), :], landing, local
     )
     mine.start()
+
+    slots = offs_ref.shape[0]
+
+    @pl.loop(0, slots)
+    def _(k):
+        here = offs_ref[pl.ds(k, 1), :]
+
+        def add(j, total):
+            same = offs_ref[pl.ds(j, 1), :] == here
+            return total + jnp.where(same, block_ref[j], 0.0)
+
+        coef_ref[k] = lax.fori_loop(0, slots, add, jnp.zeros(coef_ref.shape[1:], jnp.float32))
+
     mine.wait()
     for copy in copies:
         copy.wait_recv()
@@ -88,33 +102,37 @@
         copy.wait_send()
 
 
-def exchange_with_rims(panel):
+def exchange_with_rims(panel, offs, blocks):
     n_atom, groups = lax.axis_size("atom"), lax.axis_size("mode")
     rows, width = panel.shape[1] // groups, panel.shape[2]
     if width % 128:
         whole = lax.all_to_all(panel, "mode", split_axis=1, concat_axis=2, tiled=True)
-        return with_rims(whole, RIM)
+        return with_rims(whole, RIM), merged_blocks(offs, blocks)
+    vmem = pl.BlockSpec(memory_space=pltpu.VMEM)
     dma = pltpu.SemaphoreType.DMA
     return pl.pallas_call(
         functools.partial(exchange_kernel, n_atom, groups),
-        out_shape=jax.ShapeDtypeStruct((3, rows + 2 * RIM, width * groups), panel.dtype),
-        in_specs=[pl.BlockSpec(memory_space=pl.ANY)],
-        out_specs=pl.BlockSpec(memory_space=pl.ANY),
+        out_shape=(
+            jax.ShapeDtypeStruct((3, rows + 2 * RIM, width * groups), panel.dtype),
+            jax.ShapeDtypeStruct(blocks.shape, jnp.float32),
+        ),
+        in_specs=[pl.BlockSpec(memory_space=pl.ANY), vmem, vmem],
+        out_specs=(pl.BlockSpec(memory_space=pl.ANY), vmem),
         scratch_shapes=[dma((groups - 1,)), dma((groups - 1,)), dma((2,)), dma((2,)), dma],
         compiler_params=pltpu.CompilerParams(collective_id=1, has_side_effects=True),
         name="exchange",
-    )(panel)
-
-
-def merged_blocks(offsets, forces, displacements):
-    slots, rows = offsets.shape
+    )(panel, offs, blocks)
+
+
+def rounded_blocks(forces, displacements):
     blocks = displacements[:, :, None, None, :] * forces[:, None, :, :, :]
-    blocks = blocks.astype(jnp.bfloat16).astype(jnp.float32).reshape(slots, 9, 3, rows)
+    slots, rows = blocks.shape[0], blocks.shape[4]
+    return blocks.astype(jnp.bfloat16).astype(jnp.float32).reshape(slots, 27, rows)
+
+
+def merged_blocks(offsets, blocks):
     same = offsets[:, None, :] == offsets[None, :, :]
-    merged = jnp.sum(
-        jnp.where(same[:, :, None, None, :], blocks[None], 0.0), axis=1
-    )
-    return merged.transpose(1, 0, 2, 3).reshape(9, slots * 3, rows)
+    return jnp.sum(jnp.where(same[:, :, None, :], blocks[None], 0.0), axis=1)
 
 
 def panel_copies(groups, f_ref, panel_ref, send, recv, local):
@@ -185,7 +203,7 @@
         ),
         in_specs=[
             pl.BlockSpec((slots, BLOCK), lambda i: (0, i)),
-            pl.BlockSpec((9, slots * 3, BLOCK), lambda i: (0, 0, i)),
+            pl.BlockSpec((slots, 27, BLOCK), lambda i: (0, 0, i)),
             pl.BlockSpec(memory_space=pltpu.VMEM),
             pl.BlockSpec(memory_space=pl.ANY),
         ],
@@ -222,7 +240,7 @@
             for k in range(slots):
                 hit = here == target[k : k + 1, :]
                 for b in range(3):
-                    row = coef_ref[qa, 3 * k + b : 3 * k + b + 1, :]
+                    row = coef_ref[k, 3 * qa + b : 3 * qa + b + 1, :]
                     acc[b] = jnp.where(hit, row, acc[b])
             for b in range(3):
                 w_ref[b, pl.ds(at, CHUNK), qa * BLOCK : (qa + 1) * BLOCK] = acc[b].astype(
@@ -257,7 +275,7 @@
         out_shape=jax.ShapeDtypeStruct((9, rows, columns), jnp.bfloat16),
         in_specs=[
             pl.BlockSpec((slots, BLOCK), lambda i: (0, i)),
-            pl.BlockSpec((9, slots * 3, BLOCK), lambda i: (0, 0, i)),
+            pl.BlockSpec((slots, 27, BLOCK), lambda i: (0, 0, i)),
             pl.BlockSpec(memory_space=pltpu.VMEM),
         ],
         out_specs=pl.BlockSpec((9, BLOCK, columns), lambda i: (0, i, 0)),
@@ -436,12 +454,12 @@
     rows_dev = first_panel.shape[0] // groups
     atoms_all = first_panel.shape[0] * lax.axis_size("atom")
     scale = 1.0 / (3.0 * atoms_all) ** 0.5
-    padded = exchange_with_rims(second_panel.transpose(1, 0, 2))
     row_start = lax.axis_index("mode") * rows_dev
     shifts = lax.dynamic_slice_in_dim(offsets, row_start, rows_dev, 1)
     force_part = lax.dynamic_slice_in_dim(forces, row_start, rows_dev, 3)
     disp_part = lax.dynamic_slice_in_dim(displacements, row_start, rows_dev, 2)
-    coef = merged_blocks(shifts, force_part, disp_part)
+    blocks = rounded_blocks(force_part, disp_part)
+    padded, coef = exchange_with_rims(second_panel.transpose(1, 0, 2), shifts, blocks)
     ordered = first_panel.transpose(1, 0, 2)
     if ordered.shape[2] % 128:
         ordered, padded = lax.optimization_barrier((ordered, padded))

time: 294 us -> 282 us (0.959)
  other arithmetic: 11.2 us -> 0.32 us
  local copies, waits for them, and re-layouts: 10.3 us -> 6.22 us
  Pallas kernels: 272 us -> 275 us
    reduce_sum x1 -> x0, other arithmetic: 10.1 us -> none  [merged_blocks(): jnp.sum(jnp.where(same[:, :, None, None, :], blocks[None], 0.0), axis=1)]
    reshape x1 -> x0, local copies, waits for them, and re-layouts: 3.33 us -> none  [merged_blocks(): return merged.transpose(1, 0, 2, 3).reshape(9, slots * 3, rows)]
    transpose x1 -> x0, local copies, waits for them, and re-layouts: 3.09 us -> none  [merged_blocks(): return merged.transpose(1, 0, 2, 3).reshape(9, slots * 3, rows)]
where the time goes in v5:
time: 282 us; the launch traced here: 281 us
  Pallas kernels  275 us (98%)
  local copies, waits for them, and re-layouts  6.22 us (2%)
    pallas_call x1, Pallas kernels, make_images_and_panel(): pl.pallas_call(functools.partial(image_panel_kernel, slots, groups), grid...  111 us
    pallas_call x1, Pallas kernels, exchange_with_rims(): pl.pallas_call(functools.partial(exchange_kernel, n_atom, groups), out_sh...  92.5 us
    pallas_call x1, Pallas kernels, multiply_and_reduce(): pl.pallas_call(functools.partial(reduce_kernel, scale, n_atom, n_half), o...  71.8 us

profile of v5, /device:TPU:10, one launch (start us, length us, event | category | flops | bytes accessed | tf_op | source)
XLA Modules:
  0.0 281.4 jit_solution(9076863345412093720)
XLA Ops:
  0.0 0.0 copy-start
  0.0 1.6 constant_dynamic-slice_fusion.2.offs_ref
  1.6 0.9 constant_dynamic-slice_fusion.1
  2.5 0.0 copy-done
  2.6 0.1 multiply_convert_fusion
  2.7 0.2 bitcast_convert_fusion
  2.9 1.9 copy.8.block_ref
  4.8 92.5 %exchange.1 = (bf16[3,1024,1024]{2,1,0:T(8,128)(2,1)}, f32[24,27,512]{2,1,0:T(8,128)}) custom-call(bf16[3,4096,128]{2,1,0:T(8,128)(2,1)} %bitcast.7, s32[24,512]{1,0:T(8,128)} %constant_dynamic-slice_fusion.2.offs_ref, f32[24,27,512]{2,1,0:T(8,128)} %copy.8.block_ref), custom_call_target="tpu_custom_call" | custom-call | tf_op jit(solution)/shard_map/exchange/pallas_call | solution.py:113
  97.3 110.6 %images_panel.1 = (bf16[9,512,1024]{2,1,0:T(8,128)(2,1)}, bf16[3,512,1024]{2,1,0:T(8,128)(2,1)}) custom-call(s32[24,512]{1,0:T(8,128)} %constant_dynamic-slice_fusion.2.offs_ref, f32[24,27,512]{2,1,0:T(8,128)} %get-tuple-element.9.coef_ref, bf16[3,1024,1024]{2,1,0:T(8,128)(2,1)} %get-tuple-element.10.s_ref, bf16[3,4096,128]{2,1,0:T(8,128)(2,1)} %bitcast.8), custom_call_target="tpu_custom_call" | custom-call | tf_op jit(solution)/shard_map/images_panel/pallas_call | solution.py:197
  207.8 71.8 %reduce.1 = f32[3,32,1024]{2,1,0:T(8,128)} custom-call(bf16[3,512,1024]{2,1,0:T(8,128)(2,1)} %get-tuple-element.11.f_ref, bf16[3,3,512,1024]{3,2,1,0:T(8,128)(2,1)} %bitcast.10), custom_call_target="tpu_custom_call" | custom-call | flops 9663676416 | bytes 9437184 | tf_op jit(solution)/shard_map/reduce/pallas_call | solution.py:420
  279.6 1.8 copy.10
  (1 shorter events, 0.0 us)
Async XLA Ops:
  0.0 2.5 copy-start
